TPU v7x, 32 devices: a whole 2x2x4 slice. The times are simulated.
32 devices in a mesh: gx: 8 (over y, x, core), gy: 4 (over z).
Axes of the slice: x: 2, y: 2, z: 4, core: 2. Of those that a mesh axis runs over, the one named last changes fastest.
Arguments:
- orbitals: float32 [64, 32, 32, 128], P(None, 'gx', 'gy'), may hold values from -60 to 60, as said below
- potential: float32 [32, 32, 128], P('gx', 'gy'), may hold values from 0.2 to 2
Outputs:
- basis: float32 [64, 32, 32, 128], P(None, 'gx', 'gy')
- factor: float32 [64, 64], replicated
Inputs may be any that keep to these rules, and one draw needn't show every extreme that they name: `orbitals`: Real-valued entries.
All inputs are finite; a program needn't handle non-finite values.
Results may differ from a plain program's by a relative error of at most 0.00011.
Values sent between devices are 32-bit elements; how exact they have to be, the bound alone decides.
A program may use at most 64 MiB of HBM per device.

v0:
```python
import jax
import jax.numpy as jnp
from jax import lax
from jax.sharding import PartitionSpec as P


def extended(cells, sides, width):
    for axis, dim in sides:
        count = lax.axis_size(axis)
        head = lax.slice_in_dim(cells, 0, width, axis=dim)
        tail = lax.slice_in_dim(cells, cells.shape[dim] - width, cells.shape[dim], axis=dim)
        cells = jnp.concatenate(
            [
                lax.ppermute(tail, axis, [(i, (i + 1) % count) for i in range(count)]),
                cells,
                lax.ppermute(head, axis, [((i + 1) % count, i) for i in range(count)]),
            ],
            axis=dim,
        )
    return cells


def apply_ham(padded, pot):
    core = padded[:, 2:-2, 2:-2]
    total = -7.5 * core
    total = total + 4.0 / 3.0 * (padded[:, 3:-1, 2:-2] + padded[:, 1:-3, 2:-2])
    total = total - 1.0 / 12.0 * (padded[:, 4:, 2:-2] + padded[:, :-4, 2:-2])
    total = total + 4.0 / 3.0 * (padded[:, 2:-2, 3:-1] + padded[:, 2:-2, 1:-3])
    total = total - 1.0 / 12.0 * (padded[:, 2:-2, 4:] + padded[:, 2:-2, :-4])
    total = total + 4.0 / 3.0 * (jnp.roll(core, 1, 3) + jnp.roll(core, -1, 3))
    total = total - 1.0 / 12.0 * (jnp.roll(core, 2, 3) + jnp.roll(core, -2, 3))
    return -0.5 * total + pot[None] * core


def with_faces(field):
    return extended(field, (("gx", 1), ("gy", 2)), 2)


def upper_factor(gram):
    order = gram.shape[0]
    index = jnp.arange(order)

    def column_step(col, lower):
        row_now = lax.dynamic_slice_in_dim(lower, col, 1, 0)[0]
        target = lax.dynamic_slice_in_dim(gram, col, 1, 1)[:, 0]
        column = target - jnp.dot(
            lower, row_now, precision=lax.Precision.HIGHEST, preferred_element_type=jnp.float32
        )
        pivot = jnp.sqrt(jnp.sum(jnp.where(index == col, column, 0.0)))
        values = jnp.where(index == col, pivot, column / pivot)
        values = jnp.where(index >= col, values, 0.0)
        return jnp.where(index[None, :] == col, values[:, None], lower)

    lower = lax.fori_loop(0, order, column_step, jnp.zeros_like(gram))
    return lower.T


def upper_inverse(upper):
    order = upper.shape[0]
    index = jnp.arange(order)

    def row_step(step, inverse):
        row = order - 1 - step
        upper_row = lax.dynamic_slice_in_dim(upper, row, 1, 0)[0]
        pivot = jnp.sum(jnp.where(index == row, upper_row, 0.0))
        rest = jnp.dot(
            upper_row, inverse, precision=lax.Precision.HIGHEST, preferred_element_type=jnp.float32
        )
        unit = jnp.where(index == row, 1.0, 0.0).astype(jnp.float32)
        new_row = (unit - rest) / pivot
        return jnp.where(index[:, None] == row, new_row[None, :], inverse)

    return lax.fori_loop(0, order, row_step, jnp.zeros_like(upper))


def shards(orbitals, potential):
    first = (apply_ham(with_faces(orbitals), potential) - 5.5 * orbitals) / 4.5
    applied = apply_ham(with_faces(first), potential)
    filtered = 2.0 * (applied - 5.5 * first) / 4.5 - orbitals
    width = filtered.shape[0]
    flat = filtered.reshape(width, -1)
    cells = flat.shape[1] * lax.axis_size("gx") * lax.axis_size("gy")
    local_gram = (
        jnp.dot(flat, flat.T, precision=lax.Precision.HIGHEST, preferred_element_type=jnp.float32)
        / cells
    )
    factor = upper_factor(lax.psum(local_gram, ("gx", "gy")))
    inverse = upper_inverse(factor)
    solved = jnp.dot(
        inverse.T, flat, precision=lax.Precision.HIGHEST, preferred_element_type=jnp.float32
    )
    basis = (solved * jnp.sqrt(jnp.float32(cells))).reshape(filtered.shape)
    return (basis, factor)


def solution(mesh):
    return jax.shard_map(
        shards,
        mesh=mesh,
        in_specs=(P(None, "gx", "gy", None), P("gx", "gy", None)),
        out_specs=(P(None, "gx", "gy", None), P()),
        check_vma=False,
    )
```

profile of v0, /device:TPU:0, one launch (start us, length us, event | category | flops | bytes accessed | tf_op | source)
XLA Modules:
  0.0 343.9 jit_solution(660086592080440596)
XLA Ops:
  0.6 2.4 fusion.60
  3.0 3.3 collective-permute-start
  8.4 9.6 %collective-permute-done = f32[64,2,8,128]{3,2,1,0:T(8,128)S(1)} collective-permute-done((f32[64,2,8,128]{3,2,1,0:T(8,128)}, f32[64,2,8,128]{3,2,1,0:T(8,128)S(1)}, u32[]{:S(2)}, u32[]{:S(2)}) %collective-permute-start) | collective-permute-done | bytes 524320 | tf_op jit(solution)/shard_map/ppermute | solution.py:16
  18.3 1.6 collective-permute-done.1
  20.5 3.7 %collective-permute-start.2 = (f32[64,8,2,128]{3,1,2,0:T(8,128)S(1)}, f32[64,8,2,128]{3,1,2,0:T(8,128)S(1)}, u32[]{:S(2)}, u32[]{:S(2)}) collective-permute-start(f32[64,8,2,128]{3,1,2,0:T(8,128)S(1)} %get-tuple-element.266), channel_id=1, source_target_pairs={{1,0},{2,1},{3,2},{0,3},{5,4},{6,5},{7,6},{4,7},{9,8},{10,9},{11,1... | collective-permute-start | bytes 1572872 | tf_op jit(solution)/shard_map/ppermute | solution.py:16
  25.4 11.1 %collective-permute-done.2 = f32[64,8,2,128]{3,1,2,0:T(8,128)S(1)} collective-permute-done((f32[64,8,2,128]{3,1,2,0:T(8,128)S(1)}, f32[64,8,2,128]{3,1,2,0:T(8,128)S(1)}, u32[]{:S(2)}, u32[]{:S(2)}) %collective-permute-start.2) | collective-permute-done | bytes 524320 | tf_op jit(solution)/shard_map/ppermute | solution.py:16
  36.5 8.7 %collective-permute-done.3 = f32[64,8,2,128]{3,1,2,0:T(8,128)S(1)} collective-permute-done((f32[64,8,2,128]{3,1,2,0:T(8,128)S(1)}, f32[64,8,2,128]{3,1,2,0:T(8,128)S(1)}, u32[]{:S(2)}, u32[]{:S(2)}) %collective-permute-start.3) | collective-permute-done | bytes 524320 | tf_op jit(solution)/shard_map/ppermute | solution.py:14
  45.2 7.3 %broadcast_multiply_fusion = (f32[64,4,8,128]{3,1,2,0:T(4,128)S(1)}, f32[64,4,8,128]{3,1,2,0:T(4,128)S(1)}) fusion(f32[64,4,8,128]{3,1,2,0:T(4,128)S(1)} %copy.55, f32[4,8,128]{2,0,1:T(4,128)S(1)} %copy.71, f32[64,4,8,2]{3,1,2,0:T(4,128)S(1)} %get-tuple-element.285, f32[64,4,8,126]{3,1,2,0:T(4,128)S(1)} %get-tuple-element.287, ...), kind=kLoop, calls=%fused_computation.105 | loop fusion | flops 11796480 | bytes 9453568 | tf_op jit(solution)/shard_map/div | solution.py:77
  53.0 2.8 collective-permute-start.4
  57.3 9.6 %collective-permute-done.4 = f32[64,2,8,128]{3,2,1,0:T(8,128)S(1)} collective-permute-done((f32[64,2,8,128]{3,2,1,0:T(8,128)S(1)}, f32[64,2,8,128]{3,2,1,0:T(8,128)S(1)}, u32[]{:S(2)}, u32[]{:S(2)}) %collective-permute-start.4) | collective-permute-done | bytes 524320 | tf_op jit(solution)/shard_map/ppermute | solution.py:16
  67.2 2.6 collective-permute-done.5
  70.4 1.8 collective-permute-start.6
  73.8 10.8 %collective-permute-done.6 = f32[64,8,2,128]{3,1,2,0:T(8,128)S(1)} collective-permute-done((f32[64,8,2,128]{3,1,2,0:T(8,128)S(1)}, f32[64,8,2,128]{3,1,2,0:T(8,128)S(1)}, u32[]{:S(2)}, u32[]{:S(2)}) %collective-permute-start.6) | collective-permute-done | bytes 524320 | tf_op jit(solution)/shard_map/ppermute | solution.py:16
  84.6 8.7 %collective-permute-done.7 = f32[64,8,2,128]{3,1,2,0:T(8,128)S(1)} collective-permute-done((f32[64,8,2,128]{3,1,2,0:T(8,128)S(1)}, f32[64,8,2,128]{3,1,2,0:T(8,128)S(1)}, u32[]{:S(2)}, u32[]{:S(2)}) %collective-permute-start.7) | collective-permute-done | bytes 524320 | tf_op jit(solution)/shard_map/ppermute | solution.py:14
  93.3 7.5 %multiply_subtract_fusion = f32[64,4,8,128]{3,1,2,0:T(4,128)S(1)} fusion(f32[64,4,8,128]{3,1,2,0:T(4,128)S(1)} %get-tuple-element.261, f32[64,4,8,2]{3,1,2,0:T(4,128)S(1)} %get-tuple-element.275, f32[64,4,8,126]{3,1,2,0:T(4,128)S(1)} %get-tuple-element.277, f32[64,4,8,126]{3,1,2,0:T(4,128)S(1)} %get-tuple-element.276, ...), kind=kLoop, calls=%fused_computation.97 | loop fusion | flops 12058624 | bytes 10502144 | tf_op jit(solution)/shard_map/sub | solution.py:79
  100.8 2.1 fusion.17
  102.9 41.7 %psum.7 = f32[64,64]{1,0:T(8,128)S(1)} all-reduce(f32[64,64]{1,0:T(8,128)S(1)} %fusion.17), channel_id=1, replica_groups=mesh['gx'=8,'gy'=4] {'gx','gy'}, use_global_device_ids=true, to_apply=%region_0.1 | all-reduce | flops 4096 | bytes 32768 | tf_op jit(solution)/shard_map/psum | solution.py:87
  144.7 101.3 %while.32 = (s32[]{:T(128)}, f32[64,64]{1,0:T(8,128)S(1)}, f32[64,64]{0,1:T(8,128)S(1)}, s32[]{:T(128)}, s32[]{:T(128)}) while((s32[]{:T(128)}, f32[64,64]{1,0:T(8,128)S(1)}, f32[64,64]{0,1:T(8,128)S(1)}, s32[]{:T(128)}, s32[]{:T(128)}) %tuple.94), condition=%wide.region_3.4_spmd.clone.clone, body=%wide.region_1.3_spmd.clone.clone.sunk | while | flops 62082 | bytes 102112 | solution.py:54
  246.1 95.1 %while.31 = (s32[]{:T(128)}, f32[64,64]{1,0:T(8,128)S(1)}, f32[64,64]{1,0:T(8,128)S(1)}, s32[]{:T(128)}, s32[]{:T(128)}, /*index=5*/s32[]{:T(128)}, s32[]{:T(128)}) while((s32[]{:T(128)}, f32[64,64]{1,0:T(8,128)S(1)}, f32[64,64]{1,0:T(8,128)S(1)}, s32[]{:T(128)}, s32[]{:T(128)}, /*index=5*/s32[]{:T(128)}, s32[]{:T(128)}) %tuple.100), condition=%wide.region_6.7_spmd.clone, body=%wide.region_4.6_spmd.clone.sunk | while | flops 61958 | bytes 67106 | solution.py:73
  248.2 0.8 fusion.75
  249.7 0.8 fusion.75
  251.1 0.8 fusion.75
  252.6 0.8 fusion.75
  254.1 0.8 fusion.75
  257.1 0.8 fusion.75
  258.6 0.8 fusion.75
  260.0 0.8 fusion.75
  261.5 0.8 fusion.75
  263.0 0.8 fusion.75
  264.5 0.8 fusion.75
  266.0 0.8 fusion.75
  267.5 0.8 fusion.75
  269.0 0.8 fusion.75
  270.4 0.8 fusion.75
  271.9 0.8 fusion.75
  273.4 0.8 fusion.75
  276.4 0.8 fusion.75
  277.9 0.8 fusion.75
  279.4 0.8 fusion.75
  280.8 0.8 fusion.75
  282.3 0.8 fusion.75
  285.3 0.8 fusion.75
  286.8 0.8 fusion.75
  288.3 0.8 fusion.75
  289.8 0.8 fusion.75
  291.2 0.8 fusion.75
  292.7 0.8 fusion.75
  294.2 0.8 fusion.75
  295.7 0.8 fusion.75
  297.2 0.8 fusion.75
  298.7 0.8 fusion.75
  300.1 0.8 fusion.75
  301.6 0.8 fusion.75
  304.6 0.8 fusion.75
  306.1 0.8 fusion.75
  307.6 0.8 fusion.75
  309.1 0.8 fusion.75
  310.5 0.8 fusion.75
  313.5 0.8 fusion.75
  315.0 0.8 fusion.75
  316.5 0.8 fusion.75
  318.0 0.8 fusion.75
  341.1 1.6 fusion.16
  342.8 1.2 copy.89
  (569 shorter events, 125.2 us)
Async XLA Ops:
  0.6 5.7 %copy-start = (f32[64,4,8,128]{3,2,1,0:T(8,128)S(1)}, f32[64,4,8,128]{3,2,1,0:T(8,128)}, u32[]{:S(2)}) copy-start(f32[64,4,8,128]{3,2,1,0:T(8,128)} %param.6) | copy-start | bytes 3145732
  3.0 15.0 %collective-permute-start = (f32[64,2,8,128]{3,2,1,0:T(8,128)}, f32[64,2,8,128]{3,2,1,0:T(8,128)S(1)}, u32[]{:S(2)}, u32[]{:S(2)}) collective-permute-start(f32[64,2,8,128]{3,2,1,0:T(8,128)} %get-tuple-element.279), channel_id=1, source_target_pairs={{4,0},{8,4},{12,8},{16,12},{20,16},{24,20},{28,24},{0,28},{5,1},{9... | collective-permute-start | bytes 1572872 | tf_op jit(solution)/shard_map/ppermute | solution.py:16
  6.3 0.7 copy-start.1
  6.3 13.5 %collective-permute-start.1 = (f32[64,2,8,128]{3,2,1,0:T(8,128)}, f32[64,2,8,128]{3,2,1,0:T(8,128)S(1)}, u32[]{:S(2)}, u32[]{:S(2)}) collective-permute-start(f32[64,2,8,128]{3,2,1,0:T(8,128)} %get-tuple-element.278), channel_id=1, source_target_pairs={{0,4},{4,8},{8,12},{12,16},{16,20},{20,24},{24,28},{28,0},{1,5},{5... | collective-permute-start | bytes 1572872 | tf_op jit(solution)/shard_map/ppermute | solution.py:14
  20.5 16.0 %collective-permute-start.2 = (f32[64,8,2,128]{3,1,2,0:T(8,128)S(1)}, f32[64,8,2,128]{3,1,2,0:T(8,128)S(1)}, u32[]{:S(2)}, u32[]{:S(2)}) collective-permute-start(f32[64,8,2,128]{3,1,2,0:T(8,128)S(1)} %get-tuple-element.266), channel_id=1, source_target_pairs={{1,0},{2,1},{3,2},{0,3},{5,4},{6,5},{7,6},{4,7},{9,8},{10,9},{11,1... | collective-permute-start | bytes 1572872 | tf_op jit(solution)/shard_map/ppermute | solution.py:16
  24.1 21.1 %collective-permute-start.3 = (f32[64,8,2,128]{3,1,2,0:T(8,128)S(1)}, f32[64,8,2,128]{3,1,2,0:T(8,128)S(1)}, u32[]{:S(2)}, u32[]{:S(2)}) collective-permute-start(f32[64,8,2,128]{3,1,2,0:T(8,128)S(1)} %get-tuple-element.267), channel_id=1, source_target_pairs={{0,1},{1,2},{2,3},{3,0},{4,5},{5,6},{6,7},{7,4},{8,9},{9,10},{10,1... | collective-permute-start | bytes 1572872 | tf_op jit(solution)/shard_map/ppermute | solution.py:14
  53.0 13.9 %collective-permute-start.4 = (f32[64,2,8,128]{3,2,1,0:T(8,128)S(1)}, f32[64,2,8,128]{3,2,1,0:T(8,128)S(1)}, u32[]{:S(2)}, u32[]{:S(2)}) collective-permute-start(f32[64,2,8,128]{3,2,1,0:T(8,128)S(1)} %copy.74), channel_id=1, source_target_pairs={{4,0},{8,4},{12,8},{16,12},{20,16},{24,20},{28,24},{0,28},{5,1},{9... | collective-permute-start | bytes 1572872 | tf_op jit(solution)/shard_map/ppermute | solution.py:16
  55.9 13.9 %collective-permute-start.5 = (f32[64,2,8,128]{3,2,1,0:T(8,128)S(1)}, f32[64,2,8,128]{3,2,1,0:T(8,128)S(1)}, u32[]{:S(2)}, u32[]{:S(2)}) collective-permute-start(f32[64,2,8,128]{3,2,1,0:T(8,128)S(1)} %copy.76), channel_id=1, source_target_pairs={{0,4},{4,8},{8,12},{12,16},{16,20},{20,24},{24,28},{28,0},{1,5},{5... | collective-permute-start | bytes 1572872 | tf_op jit(solution)/shard_map/ppermute | solution.py:14
  70.4 14.2 %collective-permute-start.6 = (f32[64,8,2,128]{3,1,2,0:T(8,128)S(1)}, f32[64,8,2,128]{3,1,2,0:T(8,128)S(1)}, u32[]{:S(2)}, u32[]{:S(2)}) collective-permute-start(f32[64,8,2,128]{3,1,2,0:T(8,128)S(1)} %get-tuple-element.264), channel_id=1, source_target_pairs={{1,0},{2,1},{3,2},{0,3},{5,4},{6,5},{7,6},{4,7},{9,8},{10,9},{11,1... | collective-permute-start | bytes 1572872 | tf_op jit(solution)/shard_map/ppermute | solution.py:16
  72.2 21.1 %collective-permute-start.7 = (f32[64,8,2,128]{3,1,2,0:T(8,128)S(1)}, f32[64,8,2,128]{3,1,2,0:T(8,128)S(1)}, u32[]{:S(2)}, u32[]{:S(2)}) collective-permute-start(f32[64,8,2,128]{3,1,2,0:T(8,128)S(1)} %get-tuple-element.265), channel_id=1, source_target_pairs={{0,1},{1,2},{2,3},{3,0},{4,5},{5,6},{6,7},{7,4},{8,9},{9,10},{10,1... | collective-permute-start | bytes 1572872 | tf_op jit(solution)/shard_map/ppermute | solution.py:14
  341.1 1.6 copy-start.2
where the time goes:
time: 345 us; the launch traced here: 344 us
  matrix products  103 us (30%)
  other arithmetic  66.1 us (19%)
  waiting for transfers between devices  62.7 us (18%)
  loops' own time  46.1 us (13%)
  blocking collectives  41.7 us (12%)
  starting transfers between devices  12 us (3%)
  local copies, waits for them, and re-layouts  11.1 us (3%)
    dot_general x64, matrix products, row_step(): jnp.dot(upper_row, inverse, precision=lax.Precision.HIGHEST, preferred_el...  50.1 us
    dot_general x64, matrix products, column_step(): jnp.dot(lower, row_now, precision=lax.Precision.HIGHEST, preferred_elemen...  49.5 us
    another operation x1, loops' own time, upper_factor(): lower = lax.fori_loop(0, order, column_step, jnp.zeros_like(gram))  45.6 us
    psum x1, blocking collectives, shards(): factor = upper_factor(lax.psum(local_gram, ('gx', 'gy')))  41.7 us
    ppermute x4, waiting for transfers between devices, extended(): lax.ppermute(head, axis, [((i + 1) % count, i) for i in range(count)])  41.2 us
    reduce_sum x64, other arithmetic, row_step(): pivot = jnp.sum(jnp.where(index == row, upper_row, 0.0))  39.3 us
    ppermute x4, waiting for transfers between devices, extended(): lax.ppermute(tail, axis, [(i, (i + 1) % count) for i in range(count)])  21.6 us
    ppermute x4, starting transfers between devices, extended(): lax.ppermute(head, axis, [((i + 1) % count, i) for i in range(count)])  11.6 us
  transfers between devices with their start and end apart: 8, of which 8 were waited for; matrix products, arithmetic and copies ran while one was open for 2% of the time, Pallas kernels for 0%

commit v1 on v0

v1 whole, which is shorter than its diff:
```python
import functools

import jax
import jax.numpy as jnp
from jax import lax
from jax.experimental import pallas as pl
from jax.experimental.pallas import tpu as pltpu
from jax.sharding import PartitionSpec as P

MESH = pl.DeviceIdType.MESH
CHUNKS = 4


def pick(row, bound, a, b):
    return jnp.where(row < bound, a, b)


def pack_low(tiles, row):
    out = tiles[3]
    out = pltpu.roll(out, 6, 0)
    out = pick(row, 6, pltpu.roll(tiles[2], 4, 0), out)
    out = pick(row, 4, pltpu.roll(tiles[1], 2, 0), out)
    return pick(row, 2, tiles[0], out)


def pack_high(tiles, row):
    out = tiles[3]
    out = pick(row, 6, pltpu.roll(tiles[2], 6, 0), out)
    out = pick(row, 4, pltpu.roll(tiles[1], 4, 0), out)
    return pick(row, 2, pltpu.roll(tiles[0], 2, 0), out)


def unroll_low(packed, layer):
    return packed if layer == 0 else pltpu.roll(packed, 8 - 2 * layer, 0)


def unroll_high(packed, layer):
    return packed if layer == 3 else pltpu.roll(packed, 6 - 2 * layer, 0)


def stencil(core, below, above, ylow, yhigh, diag, row):
    near, far = -2.0 / 3.0 / 4.5, 1.0 / 24.0 / 4.5
    layers = below + core + above
    outs = []
    for x in range(4):
        c = core[x]
        top = unroll_low(ylow, x)
        bottom = unroll_high(yhigh, x)
        s1 = layers[x + 1] + layers[x + 3]
        s2 = layers[x] + layers[x + 4]
        s1 = s1 + pltpu.roll(jnp.where(row < 1, top, c), 7, 0)
        s2 = s2 + pltpu.roll(jnp.where(row < 2, top, c), 6, 0)
        s1 = s1 + pltpu.roll(jnp.where(row < 7, c, bottom), 1, 0)
        s2 = s2 + pltpu.roll(jnp.where(row < 6, c, bottom), 2, 0)
        s1 = s1 + pltpu.roll(c, 1, 1) + pltpu.roll(c, 127, 1)
        s2 = s2 + pltpu.roll(c, 2, 1) + pltpu.roll(c, 126, 1)
        outs.append(diag[x] * c + near * s1 + far * s2)
    return outs


def split3(value):
    high = value.astype(jnp.bfloat16)
    rest = value - high.astype(jnp.float32)
    middle = rest.astype(jnp.bfloat16)
    low = (rest - middle.astype(jnp.float32)).astype(jnp.bfloat16)
    return high, middle, low


def filter_kernel(
    nx, ny, orb, pot, flat_out, gram_out,
    first, filt, xlo, xhi, ylo, yhi, pklo, pkhi, gsend, grs, gsum, gex,
    xs, xr, ys, yr, rss, rsr, exs, exr, ags, agr,
):
    gx, gy = lax.axis_index("gx"), lax.axis_index("gy")
    left, right = lax.rem(gx + nx - 1, nx), lax.rem(gx + 1, nx)
    down, up = lax.rem(gy + ny - 1, ny), lax.rem(gy + 1, ny)
    width = orb.shape[0]
    size = width // CHUNKS
    row = lax.broadcasted_iota(jnp.int32, (8, 128), 0)

    barrier = pltpu.get_barrier_semaphore()
    for k in range(1, nx):
        pl.semaphore_signal(barrier, inc=1, device_id=(lax.rem(gx + k, nx), gy), device_id_type=MESH)
    for k in range(1, ny):
        pl.semaphore_signal(barrier, inc=1, device_id=(gx, lax.rem(gy + k, ny)), device_id_type=MESH)

    diag = [(pot[x] - 1.75) / 4.5 for x in range(4)]

    def pack(o, tiles, phase):
        pklo[phase, o] = pack_low(tiles, row)
        pkhi[phase, o] = pack_high(tiles, row)

    def copies(phase, chunk, source):
        span = pl.ds(chunk * size, size)
        n = (phase, chunk)
        make = pltpu.make_async_remote_copy
        return [
            make(source.at[span, 0:2], xhi.at[phase, span], xs.at[*n, 0], xr.at[*n, 0],
                 device_id=(left, gy), device_id_type=MESH),
            make(source.at[span, 2:4], xlo.at[phase, span], xs.at[*n, 1], xr.at[*n, 1],
                 device_id=(right, gy), device_id_type=MESH),
            make(pklo.at[phase, span], ylo.at[phase, span], ys.at[*n, 0], yr.at[*n, 0],
                 device_id=(gx, down), device_id_type=MESH),
            make(pkhi.at[phase, span], yhi.at[phase, span], ys.at[*n, 1], yr.at[*n, 1],
                 device_id=(gx, up), device_id_type=MESH),
        ]

    @pl.loop(0, width, unroll=4)
    def _(o):
        pack(o, [orb[o, x] for x in range(4)], 0)

    pl.semaphore_wait(barrier, nx + ny - 2)
    flights = []
    for chunk in range(CHUNKS):
        for copy in copies(0, chunk, orb):
            copy.start()
            flights.append(copy)

    for phase in range(2):
        source = (orb, first)[phase]
        for chunk in range(CHUNKS):
            for copy in copies(phase, chunk, source):
                copy.wait_recv()

            @pl.loop(chunk * size, (chunk + 1) * size, unroll=2)
            def _(o):
                tiles = stencil(
                    [source[o, x] for x in range(4)],
                    [xlo[phase, o, x] for x in range(2)],
                    [xhi[phase, o, x] for x in range(2)],
                    ylo[phase, o], yhi[phase, o], diag, row,
                )
                if phase == 0:
                    for x in range(4):
                        first[o, x] = tiles[x]
                    pack(o, tiles, 1)
                else:
                    for x in range(4):
                        filt[pl.ds(pl.multiple_of(o * 32 + 8 * x, 8), 8), :] = 2.0 * tiles[x] - orb[o, x]

            if phase == 0:
                for copy in copies(1, chunk, first):
                    copy.start()
                    flights.append(copy)

    for r in range(32):
        flat_out[:, r * 128:(r + 1) * 128] = filt[pl.ds(r, width, stride=32), :]
    gram = jnp.zeros((3 * width, 3 * width), jnp.float32)
    for step in range(8):
        parts = jnp.concatenate(split3(flat_out[:, step * 512:(step + 1) * 512]), axis=0)
        gram = gram + lax.dot_general(
            parts, parts, (((1,), (1,)), ((), ())), preferred_element_type=jnp.float32
        )
    total = jnp.zeros((width, 3 * width), jnp.float32)
    for a in (2, 1, 0):
        total = total + gram[a * width:(a + 1) * width]
    total = total[:, 2 * width:] + total[:, width:2 * width] + total[:, :width]
    cells = 4096 * nx * ny
    total = jnp.concatenate([total, jnp.zeros_like(total)], axis=1) / cells
    rows = width // nx
    for i in range(nx):
        gsend[i] = total[i * rows:(i + 1) * rows]

    step1 = []
    for k in range(1, nx):
        to = lax.rem(gx + k, nx)
        copy = pltpu.make_async_remote_copy(
            gsend.at[to], grs.at[k], rss.at[k], rsr.at[k], device_id=(to, gy), device_id_type=MESH)
        copy.start()
        step1.append(copy)
    mine = gsend[gx]
    for k in range(1, nx):
        step1[k - 1].wait_recv()
        mine = mine + grs[k]
    gex[gy] = mine
    step2 = []
    for k in range(1, ny):
        copy = pltpu.make_async_remote_copy(
            gex.at[gy], gex.at[gy], exs.at[k], exr.at[k],
            device_id=(gx, lax.rem(gy + k, ny)), device_id_type=MESH)
        copy.start()
        step2.append(copy)
    for copy in step2:
        copy.wait_recv()
    mine = gex[0]
    for j in range(1, ny):
        mine = mine + gex[j]
    gsum[gx] = mine
    step3 = []
    for k in range(1, nx):
        copy = pltpu.make_async_remote_copy(
            gsum.at[gx], gsum.at[gx], ags.at[k], agr.at[k],
            device_id=(lax.rem(gx + k, nx), gy), device_id_type=MESH)
        copy.start()
        step3.append(copy)
    for copy in step3:
        copy.wait_recv()
    for i in range(nx):
        gram_out[i * rows:(i + 1) * rows, :] = gsum[i]
    for copy in flights + step1 + step2 + step3:
        copy.wait_send()


def solve_kernel(cells, flat, gram, basis, factor):
    width = flat.shape[0]
    groups = width // 8
    lane = lax.broadcasted_iota(jnp.int32, (8, 128), 1)
    row = lax.broadcasted_iota(jnp.int32, (8, 128), 0)
    work = []
    for t in range(groups):
        unit = jnp.where(lane == row + 8 * t + width, 1.0, 0.0)
        work.append(jnp.where(lane < width, gram[8 * t:8 * t + 8, :], unit))
    for k in range(width):
        t0, r = divmod(k, 8)
        factors = [
            jnp.broadcast_to(work[t][:, k:k + 1], (8, 128)) if t >= t0 else None
            for t in range(groups)
        ]
        pivot = jnp.broadcast_to(factors[t0][r:r + 1], (8, 128))
        line = jnp.broadcast_to(work[t0][r:r + 1], (8, 128)) / pivot
        for t in range(t0, groups):
            less = factors[t] * line
            if t == t0:
                less = jnp.where(row > r, less, 0.0)
            work[t] = work[t] - less
    upper = []
    for t in range(groups):
        pivots = jnp.sum(jnp.where(lane == row + 8 * t, work[t], 0.0), axis=1, keepdims=True)
        work[t] = work[t] * (1.0 / jnp.sqrt(pivots))
        upper.append(jnp.where(lane < row + 8 * t, 0.0, work[t]))
    whole = jnp.concatenate(upper, axis=0)
    factor[...] = whole[:, :width]
    inverse = jnp.concatenate(work, axis=0)[:, width:] * (float(cells) ** 0.5)
    a, b, c = split3(inverse)
    lhs = jnp.concatenate([a, b, a, c, b, a], axis=1)
    for step in range(8):
        y1, y2, y3 = split3(flat[:, step * 512:(step + 1) * 512])
        rhs = jnp.concatenate([y1, y1, y2, y1, y2, y3], axis=0)
        out = jnp.dot(lhs, rhs, preferred_element_type=jnp.float32)
        for i in range(4):
            basis[pl.ds(step * 4 + i, width, stride=32), :] = out[:, i * 128:(i + 1) * 128]


def shards(mesh, orbitals, potential):
    nx, ny = mesh.shape["gx"], mesh.shape["gy"]
    width = orbitals.shape[0]
    local = orbitals.shape[1] * orbitals.shape[2] * orbitals.shape[3]
    rows = width // nx
    f32 = jnp.float32
    vmem = pl.BlockSpec(memory_space=pltpu.VMEM)
    dma = pltpu.SemaphoreType.DMA
    flat, gram = pl.pallas_call(
        functools.partial(filter_kernel, nx, ny),
        out_shape=[
            jax.ShapeDtypeStruct((width, local), f32),
            jax.ShapeDtypeStruct((width, 128), f32),
        ],
        in_specs=[vmem, vmem],
        out_specs=[vmem, vmem],
        scratch_shapes=[
            pltpu.VMEM(orbitals.shape, f32),
            pltpu.VMEM((width * 32, 128), f32),
            pltpu.VMEM((2, width, 2, 8, 128), f32),
            pltpu.VMEM((2, width, 2, 8, 128), f32),
            pltpu.VMEM((2, width, 8, 128), f32),
            pltpu.VMEM((2, width, 8, 128), f32),
            pltpu.VMEM((2, width, 8, 128), f32),
            pltpu.VMEM((2, width, 8, 128), f32),
            pltpu.VMEM((nx, rows, 128), f32),
            pltpu.VMEM((nx, rows, 128), f32),
            pltpu.VMEM((nx, rows, 128), f32),
            pltpu.VMEM((ny, rows, 128), f32),
            dma((2, CHUNKS, 2)), dma((2, CHUNKS, 2)), dma((2, CHUNKS, 2)), dma((2, CHUNKS, 2)),
            dma((nx,)), dma((nx,)), dma((ny,)), dma((ny,)), dma((nx,)), dma((nx,)),
        ],
        compiler_params=pltpu.CompilerParams(
            collective_id=0, has_side_effects=True, vmem_limit_bytes=32 << 20
        ),
        name="filter",
    )(orbitals, potential)
    basis, factor = pl.pallas_call(
        functools.partial(solve_kernel, local * nx * ny),
        out_shape=[
            jax.ShapeDtypeStruct((width * 32, 128), f32),
            jax.ShapeDtypeStruct((width, width), f32),
        ],
        in_specs=[vmem, vmem],
        out_specs=[vmem, vmem],
        compiler_params=pltpu.CompilerParams(vmem_limit_bytes=32 << 20),
        name="solve",
    )(flat, gram)
    return basis.reshape(orbitals.shape), factor


def solution(mesh):
    return jax.shard_map(
        functools.partial(shards, mesh),
        mesh=mesh,
        in_specs=(P(None, "gx", "gy", None), P("gx", "gy", None)),
        out_specs=(P(None, "gx", "gy", None), P()),
        check_vma=False,
    )
```

time: 345 us -> 55.2 us (0.16)
  matrix products: 103 us -> 0 us
  other arithmetic: 66.1 us -> 0 us
  waiting for transfers between devices: 62.7 us -> 0 us
  Pallas kernels: 0 us -> 52.4 us
  loops' own time: 46.1 us -> 0 us
  blocking collectives: 41.7 us -> 0 us
  starting transfers between devices: 12 us -> 0 us
  local copies, waits for them, and re-layouts: 11.1 us -> 1.93 us
    dot_general x130 -> x0, matrix products: 103 us -> none  [the longest x64 50.1 us: row_step(): jnp.dot(upper_row, inverse, precision=lax.Precision.HIGHEST, preferred_el...]
    ppermute x8 -> x0, waiting for transfers between devices: 62.7 us -> none  [the longest x4 41.2 us: extended(): lax.ppermute(head, axis, [((i + 1) % count, i) for i in range(count)])]
    pallas_call x0 -> x2, Pallas kernels: none -> 52.4 us  [the longest x1 42.1 us: shards(): pl.pallas_call(functools.partial(filter_kernel, nx, ny), out_shape=[jax.S...]
    another operation x2 -> x0, loops' own time: 46.1 us -> none  [the longest x1 45.6 us: upper_factor(): lower = lax.fori_loop(0, order, column_step, jnp.zeros_like(gram))]
    psum x1 -> x0, blocking collectives: 41.7 us -> none  [shards(): factor = upper_factor(lax.psum(local_gram, ('gx', 'gy')))]
    reduce_sum x64 -> x0, other arithmetic: 39.3 us -> none  [row_step(): pivot = jnp.sum(jnp.where(index == row, upper_row, 0.0))]
    ppermute x8 -> x0, starting transfers between devices: 12 us -> none  [the longest x4 11.6 us: extended(): lax.ppermute(head, axis, [((i + 1) % count, i) for i in range(count)])]
    select_n x192 -> x0, other arithmetic: 10.1 us -> none  [the longest x64 4.88 us: row_step(): return jnp.where(index[:, None] == row, new_row[None, :], inverse)]
  transfers between devices with their start and end apart: 8 -> 0, of which waited for: 8 -> 0; matrix products, arithmetic and copies ran while one was open for 2% -> 0% of each run, Pallas kernels for 0% -> 0%
where the time goes in v1:
time: 55.2 us; the launch traced here: 54.9 us
  Pallas kernels  52.4 us (95%)
  local copies, waits for them, and re-layouts  1.93 us (3%)
  between operations  0.65 us (1%)
    pallas_call x1, Pallas kernels, shards(): pl.pallas_call(functools.partial(filter_kernel, nx, ny), out_shape=[jax.S...  42.1 us
    pallas_call x1, Pallas kernels, shards(): pl.pallas_call(functools.partial(solve_kernel, local * nx * ny), out_shap...  10.3 us
    unnamed x4, local copies, waits for them, and re-layouts  1.93 us

profile of v1, /device:TPU:0, one launch (start us, length us, event | category | flops | bytes accessed | tf_op | source)
XLA Modules:
  0.0 54.9 jit_solution(488805208451934732)
XLA Ops:
  0.6 0.0 copy-start
  0.6 1.2 %copy-done = f32[64,4,8,128]{3,2,1,0:T(8,128)S(1)} copy-done((f32[64,4,8,128]{3,2,1,0:T(8,128)S(1)}, f32[64,4,8,128]{3,2,1,0:T(8,128)}, u32[]{:S(2)}) %copy-start) | copy-done | bytes 1048600
  1.9 0.0 copy-start.1
  1.9 0.7 %copy-done.1 = f32[4,8,128]{2,1,0:T(8,128)S(1)} copy-done((f32[4,8,128]{2,1,0:T(8,128)S(1)}, f32[4,8,128]{2,1,0:T(8,128)}, u32[]{:S(2)}) %copy-start.1) | copy-done | bytes 16408
  2.6 42.1 %filter.1 = (f32[64,4096]{1,0:T(8,128)S(1)}, f32[64,128]{1,0:T(8,128)S(1)}) custom-call(f32[64,4,8,128]{3,2,1,0:T(8,128)S(1)} %copy-done, f32[4,8,128]{2,1,0:T(8,128)S(1)} %copy-done.1), custom_call_target="tpu_custom_call" | custom-call | tf_op jit(solution)/shard_map/filter/pallas_call | solution.py:252
  44.7 10.3 %solve.1 = (f32[2048,128]{1,0:T(8,128)}, f32[64,64]{1,0:T(8,128)}) custom-call(f32[64,4096]{1,0:T(8,128)S(1)} %get-tuple-element.6.flat, f32[64,128]{1,0:T(8,128)S(1)} %get-tuple-element.7.gram), custom_call_target="tpu_custom_call" | custom-call | tf_op jit(solution)/shard_map/solve/pallas_call | solution.py:281
Async XLA Ops:
  0.6 1.2 %copy-start = (f32[64,4,8,128]{3,2,1,0:T(8,128)S(1)}, f32[64,4,8,128]{3,2,1,0:T(8,128)}, u32[]{:S(2)}) copy-start(f32[64,4,8,128]{3,2,1,0:T(8,128)} %orb.1) | copy-start | bytes 3145732
  1.9 0.7 %copy-start.1 = (f32[4,8,128]{2,1,0:T(8,128)S(1)}, f32[4,8,128]{2,1,0:T(8,128)}, u32[]{:S(2)}) copy-start(f32[4,8,128]{2,1,0:T(8,128)} %pot.1) | copy-start | bytes 49156

commit v2 on v1

--- a/solution.py
+++ b/solution.py
@@ -9,6 +9,7 @@
 
 MESH = pl.DeviceIdType.MESH
 CHUNKS = 4
+LIMIT = 52 << 20
 
 
 def pick(row, bound, a, b):
@@ -67,15 +68,22 @@
 
 
 def filter_kernel(
-    nx, ny, orb, pot, flat_out, gram_out,
-    first, filt, xlo, xhi, ylo, yhi, pklo, pkhi, gsend, grs, gsum, gex,
-    xs, xr, ys, yr, rss, rsr, exs, exr, ags, agr,
+    nx, ny, orb_hbm, pot_hbm, flat_out, gram_out,
+    orb, pot, flat, first, filt, xlo, xhi, ylo, yhi, pklo, pkhi, gsend, grs, gsum, gex,
+    lds, svs, xs, xr, ys, yr, rss, rsr, exs, exr, ags, agr,
 ):
     gx, gy = lax.axis_index("gx"), lax.axis_index("gy")
     left, right = lax.rem(gx + nx - 1, nx), lax.rem(gx + 1, nx)
     down, up = lax.rem(gy + ny - 1, ny), lax.rem(gy + 1, ny)
     width = orb.shape[0]
     size = width // CHUNKS
+    loads = [
+        pltpu.make_async_copy(
+            orb_hbm.at[c * size:(c + 1) * size], orb.at[c * size:(c + 1) * size], lds.at[c])
+        for c in range(CHUNKS)
+    ] + [pltpu.make_async_copy(pot_hbm, pot, lds.at[CHUNKS])]
+    for load in loads:
+        load.start()
     row = lax.broadcasted_iota(jnp.int32, (8, 128), 0)
 
     barrier = pltpu.get_barrier_semaphore()
@@ -84,7 +92,6 @@
     for k in range(1, ny):
         pl.semaphore_signal(barrier, inc=1, device_id=(gx, lax.rem(gy + k, ny)), device_id_type=MESH)
 
-    diag = [(pot[x] - 1.75) / 4.5 for x in range(4)]
 
     def pack(o, tiles, phase):
         pklo[phase, o] = pack_low(tiles, row)
@@ -105,16 +112,21 @@
                  device_id=(gx, up), device_id_type=MESH),
         ]
 
-    @pl.loop(0, width, unroll=4)
-    def _(o):
-        pack(o, [orb[o, x] for x in range(4)], 0)
-
-    pl.semaphore_wait(barrier, nx + ny - 2)
-    flights = []
+    flights, saves = [], []
     for chunk in range(CHUNKS):
+        loads[chunk].wait()
+
+        @pl.loop(chunk * size, (chunk + 1) * size, unroll=4)
+        def _(o):
+            pack(o, [orb[o, x] for x in range(4)], 0)
+
+        if chunk == 0:
+            pl.semaphore_wait(barrier, nx + ny - 2)
         for copy in copies(0, chunk, orb):
             copy.start()
             flights.append(copy)
+    loads[CHUNKS].wait()
+    diag = [(pot[x] - 1.75) / 4.5 for x in range(4)]
 
     for phase in range(2):
         source = (orb, first)[phase]
@@ -142,12 +154,18 @@
                 for copy in copies(1, chunk, first):
                     copy.start()
                     flights.append(copy)
-
-    for r in range(32):
-        flat_out[:, r * 128:(r + 1) * 128] = filt[pl.ds(r, width, stride=32), :]
+            else:
+                span = slice(chunk * size, (chunk + 1) * size)
+                for r in range(32):
+                    flat[span, r * 128:(r + 1) * 128] = filt[
+                        pl.ds(chunk * size * 32 + r, size, stride=32), :]
+                save = pltpu.make_async_copy(flat.at[span], flat_out.at[span], svs.at[chunk])
+                save.start()
+                saves.append(save)
+
     gram = jnp.zeros((3 * width, 3 * width), jnp.float32)
     for step in range(8):
-        parts = jnp.concatenate(split3(flat_out[:, step * 512:(step + 1) * 512]), axis=0)
+        parts = jnp.concatenate(split3(flat[:, step * 512:(step + 1) * 512]), axis=0)
         gram = gram + lax.dot_general(
             parts, parts, (((1,), (1,)), ((), ())), preferred_element_type=jnp.float32
         )
@@ -199,9 +217,13 @@
         gram_out[i * rows:(i + 1) * rows, :] = gsum[i]
     for copy in flights + step1 + step2 + step3:
         copy.wait_send()
-
-
-def solve_kernel(cells, flat, gram, basis, factor):
+    for save in saves:
+        save.wait()
+
+
+def solve_kernel(cells, flat_hbm, gram, basis, factor, flat, held, sems):
+    load = pltpu.make_async_copy(flat_hbm, flat, sems.at[4])
+    load.start()
     width = flat.shape[0]
     groups = width // 8
     lane = lax.broadcasted_iota(jnp.int32, (8, 128), 1)
@@ -210,35 +232,58 @@
     for t in range(groups):
         unit = jnp.where(lane == row + 8 * t + width, 1.0, 0.0)
         work.append(jnp.where(lane < width, gram[8 * t:8 * t + 8, :], unit))
-    for k in range(width):
-        t0, r = divmod(k, 8)
-        factors = [
-            jnp.broadcast_to(work[t][:, k:k + 1], (8, 128)) if t >= t0 else None
+    for p in range(groups):
+        spread = [
+            [jnp.broadcast_to(work[t][:, 8 * p + k:8 * p + k + 1], (8, 128)) for k in range(8)]
+            if t >= p else None
             for t in range(groups)
         ]
-        pivot = jnp.broadcast_to(factors[t0][r:r + 1], (8, 128))
-        line = jnp.broadcast_to(work[t0][r:r + 1], (8, 128)) / pivot
-        for t in range(t0, groups):
-            less = factors[t] * line
-            if t == t0:
-                less = jnp.where(row > r, less, 0.0)
-            work[t] = work[t] - less
+        block = [
+            [jnp.broadcast_to(spread[p][j][i:i + 1], (8, 128)) for j in range(i + 1)]
+            for i in range(8)
+        ]
+        lines = [jnp.broadcast_to(work[p][k:k + 1], (8, 128)) for k in range(8)]
+        roots = []
+        for k in range(8):
+            inv = 1.0 / block[k][k]
+            roots.append(1.0 / jnp.sqrt(block[k][k]))
+            scale = [block[i][k] * inv if i > k else None for i in range(8)]
+            for i in range(k + 1, 8):
+                for j in range(k + 1, i + 1):
+                    block[i][j] = block[i][j] - scale[i] * block[j][k]
+                lines[i] = lines[i] - scale[i] * lines[k]
+            for t in range(p + 1, groups):
+                column = spread[t][k]
+                for j in range(k + 1, 8):
+                    spread[t][j] = spread[t][j] - scale[j] * column
+                work[t] = work[t] - (column * inv) * lines[k]
+        tile = lines[7] * roots[7]
+        for k in range(6, -1, -1):
+            tile = jnp.where(row == k, lines[k] * roots[k], tile)
+        work[p] = tile
     upper = []
     for t in range(groups):
-        pivots = jnp.sum(jnp.where(lane == row + 8 * t, work[t], 0.0), axis=1, keepdims=True)
-        work[t] = work[t] * (1.0 / jnp.sqrt(pivots))
         upper.append(jnp.where(lane < row + 8 * t, 0.0, work[t]))
     whole = jnp.concatenate(upper, axis=0)
     factor[...] = whole[:, :width]
     inverse = jnp.concatenate(work, axis=0)[:, width:] * (float(cells) ** 0.5)
     a, b, c = split3(inverse)
     lhs = jnp.concatenate([a, b, a, c, b, a], axis=1)
-    for step in range(8):
-        y1, y2, y3 = split3(flat[:, step * 512:(step + 1) * 512])
-        rhs = jnp.concatenate([y1, y1, y2, y1, y2, y3], axis=0)
-        out = jnp.dot(lhs, rhs, preferred_element_type=jnp.float32)
-        for i in range(4):
-            basis[pl.ds(step * 4 + i, width, stride=32), :] = out[:, i * 128:(i + 1) * 128]
+    lines = held.reshape(width * 32, 128)
+    stores = []
+    load.wait()
+    for x in range(4):
+        for part in (2 * x, 2 * x + 1):
+            y1, y2, y3 = split3(flat[:, part * 512:(part + 1) * 512])
+            rhs = jnp.concatenate([y1, y1, y2, y1, y2, y3], axis=0)
+            out = jnp.dot(lhs, rhs, preferred_element_type=jnp.float32)
+            for i in range(4):
+                lines[pl.ds(part * 4 + i, width, stride=32), :] = out[:, i * 128:(i + 1) * 128]
+        store = pltpu.make_async_copy(held.at[:, 8 * x:8 * x + 8], basis.at[:, x], sems.at[x])
+        store.start()
+        stores.append(store)
+    for store in stores:
+        store.wait()
 
 
 def shards(mesh, orbitals, potential):
@@ -248,6 +293,7 @@
     rows = width // nx
     f32 = jnp.float32
     vmem = pl.BlockSpec(memory_space=pltpu.VMEM)
+    hbm = pl.BlockSpec(memory_space=pltpu.HBM)
     dma = pltpu.SemaphoreType.DMA
     flat, gram = pl.pallas_call(
         functools.partial(filter_kernel, nx, ny),
@@ -255,9 +301,12 @@
             jax.ShapeDtypeStruct((width, local), f32),
             jax.ShapeDtypeStruct((width, 128), f32),
         ],
-        in_specs=[vmem, vmem],
-        out_specs=[vmem, vmem],
+        in_specs=[hbm, hbm],
+        out_specs=[hbm, vmem],
         scratch_shapes=[
+            pltpu.VMEM(orbitals.shape, f32),
+            pltpu.VMEM(potential.shape, f32),
+            pltpu.VMEM((width, local), f32),
             pltpu.VMEM(orbitals.shape, f32),
             pltpu.VMEM((width * 32, 128), f32),
             pltpu.VMEM((2, width, 2, 8, 128), f32),
@@ -270,26 +319,28 @@
             pltpu.VMEM((nx, rows, 128), f32),
             pltpu.VMEM((nx, rows, 128), f32),
             pltpu.VMEM((ny, rows, 128), f32),
+            dma((CHUNKS + 1,)), dma((CHUNKS,)),
             dma((2, CHUNKS, 2)), dma((2, CHUNKS, 2)), dma((2, CHUNKS, 2)), dma((2, CHUNKS, 2)),
             dma((nx,)), dma((nx,)), dma((ny,)), dma((ny,)), dma((nx,)), dma((nx,)),
         ],
         compiler_params=pltpu.CompilerParams(
-            collective_id=0, has_side_effects=True, vmem_limit_bytes=32 << 20
+            collective_id=0, has_side_effects=True, vmem_limit_bytes=LIMIT
         ),
         name="filter",
     )(orbitals, potential)
     basis, factor = pl.pallas_call(
         functools.partial(solve_kernel, local * nx * ny),
         out_shape=[
-            jax.ShapeDtypeStruct((width * 32, 128), f32),
+            jax.ShapeDtypeStruct(orbitals.shape, f32),
             jax.ShapeDtypeStruct((width, width), f32),
         ],
-        in_specs=[vmem, vmem],
-        out_specs=[vmem, vmem],
-        compiler_params=pltpu.CompilerParams(vmem_limit_bytes=32 << 20),
+        in_specs=[hbm, vmem],
+        out_specs=[hbm, vmem],
+        scratch_shapes=[pltpu.VMEM((width, local), f32), pltpu.VMEM((width, 32, 128), f32), dma((5,))],
+        compiler_params=pltpu.CompilerParams(vmem_limit_bytes=16 << 20),
         name="solve",
     )(flat, gram)
-    return basis.reshape(orbitals.shape), factor
+    return basis, factor
 
 
 def solution(mesh):

time: 55.2 us -> 47.9 us (0.87)
  Pallas kernels: 52.4 us -> 46.3 us
  local copies, waits for them, and re-layouts: 1.93 us -> 0.71 us
    pallas_call x1, Pallas kernels: 10.3 us -> 4.35 us  [shards(): pl.pallas_call(functools.partial(solve_kernel, local * nx * ny), out_shap...]
    unnamed x4 -> x2, local copies, waits for them, and re-layouts: 1.93 us -> 0.71 us
where the time goes in v2:
time: 47.9 us; the launch traced here: 47.7 us
  Pallas kernels  46.3 us (97%)
  local copies, waits for them, and re-layouts  0.71 us (1%)
  between operations  0.65 us (1%)
    pallas_call x1, Pallas kernels, shards(): pl.pallas_call(functools.partial(filter_kernel, nx, ny), out_shape=[jax.S...  42 us
    pallas_call x1, Pallas kernels, shards(): pl.pallas_call(functools.partial(solve_kernel, local * nx * ny), out_shap...  4.35 us

profile of v2, /device:TPU:0, one launch (start us, length us, event | category | flops | bytes accessed | tf_op | source)
XLA Modules:
  0.0 47.7 jit_solution(8164085069665776809)
XLA Ops:
  0.6 0.0 copy-start
  0.6 0.7 %copy-done = f32[4,8,128]{2,1,0:T(8,128)S(1)} copy-done((f32[4,8,128]{2,1,0:T(8,128)S(1)}, f32[4,8,128]{2,1,0:T(8,128)}, u32[]{:S(2)}) %copy-start) | copy-done | bytes 16408
  1.3 42.0 %filter.1 = (f32[64,4096]{1,0:T(8,128)S(1)}, f32[64,128]{1,0:T(8,128)S(1)}) custom-call(f32[64,4,8,128]{3,2,1,0:T(8,128)} %orb_hbm.1, f32[4,8,128]{2,1,0:T(8,128)S(1)} %copy-done), custom_call_target="tpu_custom_call" | custom-call | tf_op jit(solution)/shard_map/filter/pallas_call | solution.py:298
  43.3 4.3 %solve.1 = (f32[64,4,8,128]{3,2,1,0:T(8,128)}, f32[64,64]{1,0:T(8,128)}) custom-call(f32[64,4096]{1,0:T(8,128)S(1)} %get-tuple-element.4.flat_hbm, f32[64,128]{1,0:T(8,128)S(1)} %get-tuple-element.5.gram), custom_call_target="tpu_custom_call" | custom-call | tf_op jit(solution)/shard_map/solve/pallas_call | solution.py:331
Async XLA Ops:
  0.6 0.7 %copy-start = (f32[4,8,128]{2,1,0:T(8,128)S(1)}, f32[4,8,128]{2,1,0:T(8,128)}, u32[]{:S(2)}) copy-start(f32[4,8,128]{2,1,0:T(8,128)} %pot_hbm.1) | copy-start | bytes 49156

commit v3 on v2

--- a/solution.py
+++ b/solution.py
@@ -134,7 +134,7 @@
             for copy in copies(phase, chunk, source):
                 copy.wait_recv()
 
-            @pl.loop(chunk * size, (chunk + 1) * size, unroll=2)
+            @pl.loop(chunk * size, (chunk + 1) * size, unroll=4)
             def _(o):
                 tiles = stencil(
                     [source[o, x] for x in range(4)],

time: 47.9 us -> 47.6 us (level)
  no operation moved by 1% of the time
where the time goes in v3:
time: 47.6 us; the launch traced here: 47.4 us
  Pallas kernels  46.1 us (97%)
  local copies, waits for them, and re-layouts  0.71 us (1%)
  between operations  0.65 us (1%)
    pallas_call x1, Pallas kernels, shards(): pl.pallas_call(functools.partial(filter_kernel, nx, ny), out_shape=[jax.S...  41.7 us
    pallas_call x1, Pallas kernels, shards(): pl.pallas_call(functools.partial(solve_kernel, local * nx * ny), out_shap...  4.36 us

profile of v3, /device:TPU:0, one launch (start us, length us, event | category | flops | bytes accessed | tf_op | source)
XLA Modules:
  0.0 47.4 jit_solution(3063496961577929215)
XLA Ops:
  0.6 0.0 copy-start
  0.6 0.7 %copy-done = f32[4,8,128]{2,1,0:T(8,128)S(1)} copy-done((f32[4,8,128]{2,1,0:T(8,128)S(1)}, f32[4,8,128]{2,1,0:T(8,128)}, u32[]{:S(2)}) %copy-start) | copy-done | bytes 16408
  1.3 41.7 %filter.1 = (f32[64,4096]{1,0:T(8,128)S(1)}, f32[64,128]{1,0:T(8,128)S(1)}) custom-call(f32[64,4,8,128]{3,2,1,0:T(8,128)} %orb_hbm.1, f32[4,8,128]{2,1,0:T(8,128)S(1)} %copy-done), custom_call_target="tpu_custom_call" | custom-call | tf_op jit(solution)/shard_map/filter/pallas_call | solution.py:298
  43.0 4.4 %solve.1 = (f32[64,4,8,128]{3,2,1,0:T(8,128)}, f32[64,64]{1,0:T(8,128)}) custom-call(f32[64,4096]{1,0:T(8,128)S(1)} %get-tuple-element.4.flat_hbm, f32[64,128]{1,0:T(8,128)S(1)} %get-tuple-element.5.gram), custom_call_target="tpu_custom_call" | custom-call | tf_op jit(solution)/shard_map/solve/pallas_call | solution.py:331
Async XLA Ops:
  0.6 0.7 %copy-start = (f32[4,8,128]{2,1,0:T(8,128)S(1)}, f32[4,8,128]{2,1,0:T(8,128)}, u32[]{:S(2)}) copy-start(f32[4,8,128]{2,1,0:T(8,128)} %pot_hbm.1) | copy-start | bytes 49156
